TPU v7x, 256 devices: a whole 4x4x8 slice. The times are simulated.
256 devices in a mesh: dp: 4 (over x), expert: 64 (over y, z, core).
Axes of the slice: x: 4, y: 4, z: 8, core: 2. Of those that a mesh axis runs over, the one named last changes fastest.
Arguments:
- tokens: bfloat16 [8192, 3584], P(('dp', 'expert')), may hold values from -6 to 6
- routes: int32 [8192, 8], P(('dp', 'expert')), may hold values from 0 to 127, all different within a row; in each aligned block of 32 rows (0 to 31, 32 to 63, ...) at most 4 rows name the same one
- route_weight: float32 [8192, 8], P(('dp', 'expert')), may hold values from 0.1 to 1
- gate_weight: bfloat16 [128, 3584, 1024], P('expert', None, 'dp'), may hold values from -0.09375 to 0.09375
- up_weight: bfloat16 [128, 3584, 1024], P('expert', None, 'dp'), may hold values from -0.09375 to 0.09375
- down_weight: bfloat16 [128, 1024, 3584], P('expert', 'dp'), may hold values from -0.1875 to 0.1875
- gate_scale: float32 [128, 28, 8], P('expert', None, 'dp'), may hold values from 0.5 to 2
- up_scale: float32 [128, 28, 8], P('expert', None, 'dp'), may hold values from 0.5 to 2
- down_scale: float32 [128, 8, 28], P('expert', 'dp'), may hold values from 0.5 to 2
Outputs:
- mixed: bfloat16 [8192, 3584], P(('dp', 'expert'))
- load_share: float32 [128], replicated
Inputs may be any that keep to these rules, and one draw needn't show every extreme that they name: `routes`: each row names 8 different experts. Within the rows of one device (32 aligned rows) no expert is named by more than 4 rows, and in every draw some expert is named by exactly 4 rows of some device.
All inputs are finite; a program needn't handle non-finite values.
Results may differ from a plain program's by a relative error of at most 0.015.
Values may be sent and summed in bfloat16 or wider, within the bound.
No kernel may reach another device: no remote copies, remote signals or barrier semaphores. Data moves between devices by JAX's collectives and lax.ppermute only.
A program may use at most 192 MiB of HBM per device.

v0:
```python
import jax
import jax.numpy as jnp
from jax import lax
from jax.sharding import PartitionSpec as P

HOT = 2
BLOCK = 128


def dequantize(weight, block_scale):
    groups, rows_all, cols_all = weight.shape
    blocks = weight.astype(jnp.float32).reshape(
        groups, rows_all // BLOCK, BLOCK, cols_all // BLOCK, BLOCK
    )
    blocks = blocks * block_scale[:, :, None, :, None]
    return blocks.reshape(groups, rows_all, cols_all).astype(jnp.bfloat16)


def expert_part(token_rows, gate_deq, up_deq, down_deq):
    flat_rows = token_rows[0]
    gate_val = jnp.einsum("grd,gdf->grf", flat_rows, gate_deq, preferred_element_type=jnp.float32)
    up_val = jnp.einsum("grd,gdf->grf", flat_rows, up_deq, preferred_element_type=jnp.float32)
    hidden = (jax.nn.silu(gate_val) * up_val).astype(jnp.bfloat16)
    return jnp.einsum("grf,gfd->grd", hidden, down_deq, preferred_element_type=jnp.float32)[None]


def spread_sum(token_rows, gate_deq, up_deq, down_deq):
    term_sums = expert_part(
        lax.all_gather(token_rows, "dp", axis=2, tiled=True), gate_deq, up_deq, down_deq
    )
    return lax.psum_scatter(
        term_sums.astype(jnp.bfloat16), "dp", scatter_dimension=2, tiled=True
    ).astype(jnp.float32)


def send_out(buffer):
    return lax.all_to_all(buffer, "expert", split_axis=0, concat_axis=2, tiled=True)


def send_back(result):
    return lax.all_to_all(result, "expert", split_axis=2, concat_axis=0, tiled=True)


def per_device(
    tokens,
    routes,
    route_weight,
    gate_weight,
    up_weight,
    down_weight,
    gate_scale,
    up_scale,
    down_scale,
):
    tok_rows, model_width = tokens.shape
    top_count = routes.shape[1]
    local_experts = gate_weight.shape[0]
    groups = lax.axis_size("expert")
    experts = local_experts * groups
    total_rows = tok_rows * lax.axis_size("dp") * groups
    capacity_cold = min(tok_rows - 1, max(2, tok_rows * top_count // experts + 1))
    gate_deq = dequantize(gate_weight, gate_scale)
    up_deq = dequantize(up_weight, up_scale)
    down_deq = dequantize(down_weight, down_scale)
    labels = jnp.arange(experts, dtype=jnp.int32)
    per_row = jnp.sum((routes[:, :, None] == labels[None, None, :]).astype(jnp.int32), axis=1)
    load_totals = lax.psum(jnp.sum(per_row, axis=0), ("dp", "expert"))
    load_share = load_totals.astype(jnp.float32) * (experts / (total_rows * top_count))
    _, hot_ids = lax.top_k(load_totals * experts + (experts - 1 - labels), HOT)
    before = jnp.cumsum(per_row, axis=0) - per_row
    rank_index = jnp.take_along_axis(before, routes, axis=1)
    hot_match = routes[:, :, None] == hot_ids[None, None, :]
    is_hot = jnp.any(hot_match, axis=-1)
    kept_mask = is_hot | (rank_index < capacity_cold)
    slots_cap = capacity_cold + 1
    slot_index = jnp.where(kept_mask, routes * slots_cap + rank_index, experts * slots_cap).reshape(
        -1
    )
    copies = jnp.broadcast_to(tokens[:, None, :], (tok_rows, top_count, model_width)).reshape(
        -1, model_width
    )
    buffer = (
        jnp.zeros((experts * slots_cap + 1, model_width), jnp.bfloat16).at[slot_index].set(copies)
    )
    buffer = buffer[:-1].reshape(groups, local_experts, slots_cap, model_width)
    arrived = send_out(buffer)
    results = send_back(spread_sum(arrived, gate_deq, up_deq, down_deq).astype(jnp.bfloat16))
    result_table = jnp.concatenate(
        [results.reshape(-1, model_width), jnp.zeros((1, model_width), jnp.bfloat16)], axis=0
    )
    outputs = result_table[slot_index].reshape(tok_rows, top_count, model_width).astype(jnp.float32)
    weights = jnp.where(kept_mask, route_weight, 0.0)
    combined = jnp.sum(weights[:, :, None] * outputs, axis=1)
    return (combined.astype(jnp.bfloat16), load_share)


def solution(mesh):
    in_specs = (
        P(("dp", "expert"), None),
        P(("dp", "expert"), None),
        P(("dp", "expert"), None),
        P("expert", None, "dp"),
        P("expert", None, "dp"),
        P("expert", "dp", None),
        P("expert", None, "dp"),
        P("expert", None, "dp"),
        P("expert", "dp", None),
    )
    out_specs = (P(("dp", "expert"), None), P())
    return jax.shard_map(
        per_device, mesh=mesh, in_specs=in_specs, out_specs=out_specs, check_vma=False
    )
```

profile of v0, /device:TPU:8, one launch (start us, length us, event | category | flops | bytes accessed | tf_op | source)
XLA Modules:
  0.0 649.7 jit_solution(4077205381951862050)
XLA Ops:
  11.2 78.5 %psum.7 = s32[128]{0:T(128)S(1)} all-reduce(s32[128]{0:T(128)S(1)} %get-tuple-element.6), channel_id=1, replica_groups=mesh['dp'=4,'expert'=64] {'dp','expert'}, use_global_device_ids=true, to_apply=%region_1.0 | all-reduce | flops 128 | bytes 1024 | tf_op jit(solution)/shard_map/psum | solution.py:67
  92.5 5.5 scatter_custom_fusion
  98.0 4.1 slice.10
  102.1 7.0 %reshape.77 = bf16[64,2,4,3584]{3,2,1,0:T(4,128)(2,1)} reshape(bf16[512,3584]{1,0:T(8,128)(2,1)} %slice.10) | data formatting | bytes 7340032 | tf_op jit(solution)/shard_map/reshape | solution.py:85
  109.1 91.7 %all_to_all.33 = bf16[64,2,4,3584]{3,2,1,0:T(4,128)(2,1)S(1)} all-to-all(bf16[64,2,4,3584]{3,2,1,0:T(4,128)(2,1)} %reshape.77), channel_id=1, replica_groups=mesh['dp'=4,'expert'=64] {'expert'}, dimensions={0} | all-to-all | bytes 7340032 | tf_op jit(solution)/shard_map/all_to_all | solution.py:37
  203.9 6.8 %all_to_all.27 = bf16[1,2,256,3584]{3,2,1,0:T(8,128)(2,1)} reshape(bf16[1,2,64,4,3584]{4,3,2,1,0:T(4,128)(2,1)} %copy.51) | data formatting | bytes 7340032 | tf_op jit(solution)/shard_map/all_to_all | solution.py:37
  211.4 4.9 mul.71
  216.4 11.3 %mul.72 = f32[2,3584,256]{2,1,0:T(8,128)} reshape(f32[2,28,128,2,128]{4,3,2,1,0:T(2,128)} %mul.71) | data formatting | bytes 14680064 | tf_op jit(solution)/shard_map/mul | solution.py:15
  227.7 4.9 mul.75
  232.7 10.5 %mul.76 = f32[2,3584,256]{2,1,0:T(8,128)} reshape(f32[2,28,128,2,128]{4,3,2,1,0:T(2,128)} %mul.75) | data formatting | bytes 14680064 | tf_op jit(solution)/shard_map/mul | solution.py:15
  243.2 5.0 mul.79
  248.2 10.5 %mul.80 = f32[2,256,3584]{1,2,0:T(8,128)} reshape(f32[2,2,128,28,128]{2,1,4,3,0:T(2,128)} %mul.79) | data formatting | bytes 14680064 | tf_op jit(solution)/shard_map/mul | solution.py:15
  258.7 6.0 copy.54
  264.7 81.2 %all-gather.2.cloned.1.call-done = bf16[1,2,1024,3584]{3,2,1,0:T(8,128)(2,1)} async-done(((bf16[1,2,256,3584]{3,2,1,0:T(8,128)(2,1)}), bf16[1,2,1024,3584]{3,2,1,0:T(8,128)(2,1)}) %all-gather.2.cloned.1.call-update) | async-done | bytes 14680080 | tf_op jit(solution)/shard_map/all_gather | solution.py:29
  346.0 10.4 %fusion.2 = f32[2,1024,256]{2,1,0:T(8,128)S(1)} fusion(bf16[1,2,1024,3584]{3,2,1,0:T(8,128)(2,1)} %all-gather.2.cloned.1.call-done, f32[2,3584,256]{2,1,0:T(8,128)} %mul.72, bf16[2,3584,256]{2,1,0:T(8,128)(2,1)} %param.12), kind=kOutput, calls=%fused_computation.5 | convolution fusion | flops 3763601408 | bytes 27787264 | tf_op jit(solution)/shard_map/grd,gdf->grf/dot_general | solution.py:21
  356.4 12.5 %multiply_convert_fusion.6 = bf16[2,1024,256]{2,1,0:T(8,128)(2,1)S(1)} fusion(f32[2,1024,256]{2,1,0:T(8,128)S(1)} %fusion.2, f32[2,3584,256]{2,1,0:T(8,128)} %mul.76, bf16[2,3584,256]{2,1,0:T(8,128)(2,1)} %param.13, bf16[1,2,1024,3584]{3,2,1,0:T(8,128)(2,1)} %all-gather.2.cloned.1.call-done), kind=kOutput, calls=%fused_computation.14 | convolution fusion | flops 3766747136 | bytes 28835840 | tf_op jit(solution)/shard_map/grd,gdf->grf/dot_general | solution.py:22
  368.9 11.7 %convert_bitcast_fusion = bf16[1,2,1024,3584]{3,2,1,0:T(8,128)(2,1)} fusion(bf16[2,1024,256]{2,1,0:T(8,128)(2,1)S(1)} %multiply_convert_fusion.6, f32[2,256,3584]{1,2,0:T(8,128)} %mul.80, bf16[2,256,3584]{1,2,0:T(8,128)(2,1)} %copy.54), kind=kOutput, calls=%fused_computation.7 | convolution fusion | flops 3770941440 | bytes 26738688 | tf_op jit(solution)/shard_map/grf,gfd->grd/dot_general | solution.py:24
  380.6 135.2 %reduce-scatter.2.cloned.1.call-done = bf16[1,2,256,3584]{3,2,1,0:T(8,128)(2,1)} async-done(((bf16[1,2,1024,3584]{3,2,1,0:T(8,128)(2,1)}), bf16[1,2,256,3584]{3,2,1,0:T(8,128)(2,1)}) %reduce-scatter.2.cloned.1.call-update) | async-done | bytes 3670032 | tf_op jit(solution)/shard_map/reduce_scatter | solution.py:31
  515.8 7.6 %copy.57 = bf16[1,2,256,3584]{3,1,0,2:T(2,128)(2,1)} copy(bf16[1,2,256,3584]{3,2,1,0:T(8,128)(2,1)} %reduce-scatter.2.cloned.1.call-done) | data formatting | bytes 7340032 | tf_op jit(solution)/shard_map/reduce_scatter | solution.py:31
  523.5 11.3 %all-to-all-start.1 = ((bf16[1,2,256,3584]{3,1,0,2:T(2,128)(2,1)}), bf16[1,2,256,3584]{3,1,0,2:T(2,128)(2,1)}, u32[]{:S(2)}, u32[]{:S(2)}) async-start(bf16[1,2,256,3584]{3,1,0,2:T(2,128)(2,1)} %copy.57), calls=%async_computation.2 | async-start | bytes 7340032 | tf_op jit(solution)/shard_map/all_to_all | solution.py:41
  535.3 82.9 %all-to-all-done.1 = bf16[1,2,256,3584]{3,1,0,2:T(2,128)(2,1)} async-done(((bf16[1,2,256,3584]{3,1,0,2:T(2,128)(2,1)}), bf16[1,2,256,3584]{3,1,0,2:T(2,128)(2,1)}, u32[]{:S(2)}, u32[]{:S(2)}) %all-to-all-start.1) | async-done | bytes 3670048 | tf_op jit(solution)/shard_map/all_to_all | solution.py:41
  618.2 5.3 copy.61
  623.5 6.7 %reshape.78 = bf16[512,3584]{1,0:T(8,128)(2,1)} reshape(bf16[64,1,2,4,3584]{4,3,2,0,1:T(4,128)(2,1)} %bitcast.34) | data formatting | bytes 7340032 | tf_op jit(solution)/shard_map/reshape | solution.py:89
  634.4 6.1 gather_fusion
  (46 shorter events, 17.7 us)
Async XLA Ops:
  7.2 85.3 %copy-start = (bf16[32,3584]{1,0:T(8,128)(2,1)S(1)}, bf16[32,3584]{1,0:T(8,128)(2,1)}, u32[]{:S(2)}) copy-start(bf16[32,3584]{1,0:T(8,128)(2,1)} %param.9) | copy-start | bytes 688132
  7.2 338.8 %all-gather.2.cloned.1.call-start = ((), (), s32[]{:S(2)}) async-start(), calls=%async_computation.3 | async-start | bytes 18350080 | tf_op jit(solution)/shard_map/all_gather | solution.py:29
  9.1 83.1 %copy-start.2 = (s32[32,8]{0,1:T(8,128)S(1)}, s32[32,8]{0,1:T(8,128)}, u32[]{:S(2)}) copy-start(s32[32,8]{0,1:T(8,128)} %param.10) | copy-start | bytes 3076
  210.6 0.7 copy-start.4
  210.7 305.1 %reduce-scatter.2.cloned.1.call-start = ((), (), s32[]{:S(2)}) async-start(), calls=%async_computation.4 | async-start | bytes 18350080 | tf_op jit(solution)/shard_map/reduce_scatter | solution.py:31
  216.4 11.3 %copy-start.5 = (f32[2,28,2]{1,2,0:T(2,128)S(1)}, f32[2,28,2]{1,2,0:T(2,128)}, u32[]{:S(2)}) copy-start(f32[2,28,2]{1,2,0:T(2,128)} %param.16) | copy-start | bytes 1348
  232.7 10.5 %copy-start.6 = (f32[2,2,28]{2,1,0:T(2,128)S(1)}, f32[2,2,28]{2,1,0:T(2,128)}, u32[]{:S(2)}) copy-start(f32[2,2,28]{2,1,0:T(2,128)} %param.17) | copy-start | bytes 1348
  523.4 11.3 %copy-start.3 = (f32[32,8]{0,1:T(8,128)S(1)}, f32[32,8]{0,1:T(8,128)}, u32[]{:S(2)}) copy-start(f32[32,8]{0,1:T(8,128)} %param.11) | copy-start | bytes 3076
  523.5 94.8 %all-to-all-start.1 = ((bf16[1,2,256,3584]{3,1,0,2:T(2,128)(2,1)}), bf16[1,2,256,3584]{3,1,0,2:T(2,128)(2,1)}, u32[]{:S(2)}, u32[]{:S(2)}) async-start(bf16[1,2,256,3584]{3,1,0,2:T(2,128)(2,1)} %copy.57), calls=%async_computation.2 | async-start | bytes 7340032 | tf_op jit(solution)/shard_map/all_to_all | solution.py:41
  634.4 8.3 %copy-start.1 = (bf16[32,3584]{1,0:T(8,128)(2,1)S(1)}, bf16[32,3584]{1,0:T(8,128)(2,1)}, u32[]{:S(2)}) copy-start(bf16[32,3584]{1,0:T(8,128)(2,1)} %param.9) | copy-start | bytes 688132
Sparse Core Ops, SparseCore 0:
  210.8 135.1 all-gather.1
  380.8 135.0 reduce-scatter.1
where the time goes:
time: 662 us; the launch traced here: 650 us
  waiting for transfers between devices  299 us (45%)
  blocking collectives  170 us (26%)
  local copies, waits for them, and re-layouts  114 us (17%)
  matrix products  34.6 us (5%)
  between operations  14.4 us (2%)
  starting transfers between devices  11.3 us (2%)
    reduce_scatter x1, waiting for transfers between devices, spread_sum(): lax.psum_scatter(term_sums.astype(jnp.bfloat16), 'dp', scatter_dimension=...  135 us
    all_to_all x1, blocking collectives, send_out(): lax.all_to_all(buffer, 'expert', split_axis=0, concat_axis=2, tiled=True)  91.7 us
    all_to_all x1, waiting for transfers between devices, send_back(): lax.all_to_all(result, 'expert', split_axis=2, concat_axis=0, tiled=True)  82.9 us
    all_gather x1, waiting for transfers between devices, spread_sum(): lax.all_gather(token_rows, 'dp', axis=2, tiled=True)  81.2 us
    psum x1, blocking collectives, per_device(): load_totals = lax.psum(jnp.sum(per_row, axis=0), ('dp', 'expert'))  78.5 us
    mul x6, local copies, waits for them, and re-layouts, dequantize(): blocks = blocks * block_scale[:, :, None, :, None]  47 us
  transfers between devices with their start and end apart: 3, of which 3 were waited for; matrix products, arithmetic and copies ran while one was open for 8% of the time, Pallas kernels for 0%

commit v1 on v0

v1 whole, which is shorter than its diff:
```python
import functools

import jax
import jax.numpy as jnp
from jax import lax
from jax.experimental import pallas as pl
from jax.experimental.pallas import tpu as pltpu
from jax.sharding import PartitionSpec as P

BLOCK = 128
CAP = 3
NY, NZ, NC, NX = 4, 8, 2, 4
SRC = NZ * NC
PIECE = SRC * CAP
META = 128
COLS = 512
BF = jnp.bfloat16
F32 = jnp.float32
VMEM = 48 * 1024 * 1024


def expert_move(value, dy=0, dz=0, flip=False, xor_y=0):
    pairs = []
    for y in range(NY):
        for z in range(NZ):
            for c in range(NC):
                to_y = (y + dy) % NY ^ xor_y
                to_z = (z + dz) % NZ
                to_c = c ^ 1 if flip else c
                pairs.append(((y * NZ + z) * NC + c, (to_y * NZ + to_z) * NC + to_c))
    return lax.ppermute(value, "expert", pairs)


def dp_move(value, dx=0, xor_x=0):
    return lax.ppermute(value, "dp", [(x, (x + dx) % NX ^ xor_x) for x in range(NX)])


def slot_values(metas, lanes):
    tokens = metas.shape[0]
    found = jnp.zeros((tokens, META), F32)
    for k in range(8):
        found += jnp.where(metas[:, k : k + 1] == lanes, 1.0, 0.0)
    row = lax.broadcasted_iota(jnp.int32, (tokens, tokens), 0)
    col = lax.broadcasted_iota(jnp.int32, (tokens, tokens), 1)
    earlier = jnp.where(((row >> 5) == (col >> 5)) & (col < row), 1.0, 0.0).astype(BF)
    rank = jnp.dot(earlier, found.astype(BF), preferred_element_type=F32)
    return found * (rank + 1.0)


def slot_parts(slots):
    lane = (slots * 1366) >> 16
    rest = slots - lane * PIECE
    return lane, rest >> 4, rest & 15


def gather_kernel(lanes_ref, *refs):
    pieces, outs, counts_ref = refs[:SRC], refs[SRC : SRC + 8], refs[SRC + 8]
    tokens, slots = SRC * 32, 8 * PIECE
    depth = outs[0].shape[1]
    metas = jnp.concatenate([p[:, depth : depth + META] for p in pieces], axis=0).astype(F32)
    values = slot_values(metas, lanes_ref[0:1, :])
    every = lax.broadcasted_iota(jnp.int32, (1, META), 1).astype(F32)
    total = jnp.zeros((tokens, META), F32)
    for k in range(8):
        total += jnp.where(metas[:, k : k + 1] == every, 1.0, 0.0)
    counts_ref[...] = jnp.broadcast_to(jnp.sum(total, axis=0, keepdims=True), (8, META))
    slot_lane, _, _ = slot_parts(lax.broadcasted_iota(jnp.int32, (slots, META), 0))
    spread = jnp.where(
        slot_lane == lax.broadcasted_iota(jnp.int32, (slots, META), 1), 1.0, 0.0
    ).astype(BF)
    picked = lax.dot_general(
        spread, values.astype(BF), (((1,), (1,)), ((), ())), preferred_element_type=F32
    )
    _, rank, source = slot_parts(lax.broadcasted_iota(jnp.int32, (slots, tokens), 0))
    token = lax.broadcasted_iota(jnp.int32, (slots, tokens), 1)
    choose = jnp.where(
        (picked == (rank + 1).astype(F32)) & (source == (token >> 5)), 1.0, 0.0
    ).astype(BF)
    for start in range(0, depth, COLS):
        block = jnp.concatenate([p[:, start : start + COLS] for p in pieces], axis=0)
        rows = jnp.dot(choose, block, preferred_element_type=F32).astype(BF)
        for j in range(8):
            outs[j][:, start : start + COLS] = rows[j * PIECE : (j + 1) * PIECE]


def scatter_kernel(lanes_ref, *refs):
    pieces, rows_in = refs[:SRC], refs[SRC : SRC + 8]
    own_ref, other_ref = refs[SRC + 8 :]
    tokens, slots = SRC * 32, 8 * PIECE
    depth = own_ref.shape[1]
    lanes = lanes_ref[0:1, :]
    metas = jnp.concatenate([p[:, depth : depth + META] for p in pieces], axis=0).astype(F32)
    values = slot_values(metas, lanes)
    high = jnp.zeros((tokens, META), F32)
    low = jnp.zeros((tokens, META), F32)
    for k in range(8):
        match = metas[:, k : k + 1] == lanes
        high += jnp.where(match, metas[:, 8 + k : 9 + k], 0.0)
        low += jnp.where(match, metas[:, 16 + k : 17 + k], 0.0)
    slot_lane, _, _ = slot_parts(lax.broadcasted_iota(jnp.int32, (META, slots), 1))
    spread = jnp.where(
        slot_lane == lax.broadcasted_iota(jnp.int32, (META, slots), 0), 1.0, 0.0
    ).astype(BF)
    picked = jnp.dot(values.astype(BF), spread, preferred_element_type=F32)
    _, rank, source = slot_parts(lax.broadcasted_iota(jnp.int32, (tokens, slots), 1))
    token = lax.broadcasted_iota(jnp.int32, (tokens, slots), 0)
    there = (picked == (rank + 1).astype(F32)) & (source == (token >> 5))
    high_at = jnp.dot(high.astype(BF), spread, preferred_element_type=F32)
    low_at = jnp.dot(low.astype(BF), spread, preferred_element_type=F32)
    high_at = jnp.where(there, high_at, 0.0).astype(BF)
    low_at = jnp.where(there, low_at, 0.0).astype(BF)
    half = tokens // 2
    for start in range(0, depth, COLS):
        block = jnp.concatenate([r[:, start : start + COLS] for r in rows_in], axis=0)
        sums = jnp.dot(high_at, block, preferred_element_type=F32)
        sums += jnp.dot(low_at, block, preferred_element_type=F32)
        sums = sums.astype(BF)
        own_ref[:, start : start + COLS] = sums[:half]
        other_ref[:, start : start + COLS] = sums[half:]


def whole(count):
    return [pl.BlockSpec(memory_space=pltpu.VMEM)] * count


def gather_rows(lanes, pieces, depth):
    out = [jax.ShapeDtypeStruct((PIECE, depth), BF)] * 8
    return pl.pallas_call(
        gather_kernel,
        out_shape=out + [jax.ShapeDtypeStruct((8, META), F32)],
        in_specs=whole(1 + SRC),
        out_specs=whole(9),
        compiler_params=pltpu.CompilerParams(vmem_limit_bytes=VMEM),
        cost_estimate=pl.CostEstimate(
            flops=2 * 384 * 512 * depth, bytes_accessed=7 * 1024 * 1024, transcendentals=0
        ),
        name="gather_rows",
    )(lanes, *pieces)


def scatter_rows(lanes, pieces, rows, depth):
    return pl.pallas_call(
        scatter_kernel,
        out_shape=[jax.ShapeDtypeStruct((SRC * 16, depth), BF)] * 2,
        in_specs=whole(1 + SRC + 8),
        out_specs=whole(2),
        compiler_params=pltpu.CompilerParams(vmem_limit_bytes=VMEM),
        cost_estimate=pl.CostEstimate(
            flops=4 * 384 * 512 * depth, bytes_accessed=10 * 1024 * 1024, transcendentals=0
        ),
        name="scatter_rows",
    )(lanes, *pieces, *rows)


def ffn_kernel(in_rows, out_rows, steps, masked, *refs):
    refs = list(refs)
    flags = refs.pop(0) if masked else None
    xs, refs = refs[: len(in_rows)], refs[len(in_rows) :]
    gate_w, up_w, down_w, gate_s, up_s, down_s = refs[:6]
    outs, (gate_acc, up_acc, hidden) = refs[6 : 6 + len(out_rows)], refs[6 + len(out_rows) :]
    step = pl.program_id(0)
    blocks = COLS // BLOCK

    def deq(w_ref, s_ref):
        parts = []
        for b in range(blocks):
            scale = s_ref[0, pl.ds(step * blocks + b, 1), :]
            part = w_ref[0, b * BLOCK : (b + 1) * BLOCK, :].astype(F32) * scale
            parts.append(part.astype(BF))
        return jnp.concatenate(parts, axis=0)

    @pl.when(step < steps)
    def _():
        x = jnp.concatenate([r[...] for r in xs], axis=0)
        gate = jnp.dot(x, deq(gate_w, gate_s), preferred_element_type=F32)
        up = jnp.dot(x, deq(up_w, up_s), preferred_element_type=F32)

        @pl.when(step == 0)
        def _():
            gate_acc[...] = gate
            up_acc[...] = up

        @pl.when(step > 0)
        def _():
            gate_acc[...] += gate
            up_acc[...] += up

    @pl.when(step == steps)
    def _():
        gate = gate_acc[...]
        value = gate * (1.0 / (1.0 + jnp.exp(-gate))) * up_acc[...]
        if masked:
            odd = lax.broadcasted_iota(jnp.int32, value.shape, 0) & 1
            value = jnp.where(jnp.where(odd == 1, flags[1], flags[0]) == 1, value, 0.0)
        hidden[...] = value.astype(BF)

    @pl.when(step >= steps)
    def _():
        parts = []
        for b in range(down_w.shape[1] // BLOCK):
            part = down_w[0, b * BLOCK : (b + 1) * BLOCK, :].astype(F32) * down_s[0, b : b + 1, :]
            parts.append(part.astype(BF))
        result = jnp.dot(
            hidden[...], jnp.concatenate(parts, axis=0), preferred_element_type=F32
        ).astype(BF)
        at = 0
        for ref, count in zip(outs, out_rows):
            ref[...] = result[at : at + count]
            at += count


def ffn(xs, out_rows, which, weights, flags=None):
    gate_w, up_w, down_w, gate_s, up_s, down_s = weights
    depth, units = gate_w.shape[1:]
    steps = depth // COLS
    in_rows = [x.shape[0] for x in xs]
    total = sum(in_rows)
    masked = flags is not None

    def early(i):
        return jnp.minimum(i, steps - 1)

    def late(i):
        return jnp.maximum(i - steps, 0)

    in_specs = [pl.BlockSpec(memory_space=pltpu.SMEM)] if masked else []
    in_specs += [pl.BlockSpec((r, COLS), lambda i: (0, early(i))) for r in in_rows]
    in_specs += [pl.BlockSpec((1, COLS, units), lambda i: (which, early(i), 0))] * 2
    in_specs += [pl.BlockSpec((1, units, COLS), lambda i: (which, 0, late(i)))]
    in_specs += [pl.BlockSpec((1,) + gate_s.shape[1:], lambda i: (which, 0, 0))] * 2
    in_specs += [pl.BlockSpec((1, down_s.shape[1], COLS), lambda i: (which, 0, late(i)))]
    return pl.pallas_call(
        functools.partial(ffn_kernel, in_rows, out_rows, steps, masked),
        grid=(2 * steps,),
        out_shape=[jax.ShapeDtypeStruct((r, depth), BF) for r in out_rows],
        in_specs=in_specs,
        out_specs=[pl.BlockSpec((r, COLS), lambda i: (0, late(i))) for r in out_rows],
        scratch_shapes=[
            pltpu.VMEM((total, units), F32),
            pltpu.VMEM((total, units), F32),
            pltpu.VMEM((total, units), BF),
        ],
        compiler_params=pltpu.CompilerParams(vmem_limit_bytes=VMEM),
        cost_estimate=pl.CostEstimate(
            flops=6 * total * units * depth,
            bytes_accessed=4 * total * depth + 6 * units * depth,
            transcendentals=total * units,
        ),
        name="ffn",
    )(*((flags,) if masked else ()), *xs, gate_w, up_w, down_w, gate_s, up_s, down_s)


def add(*values):
    total = values[0].astype(F32)
    for value in values[1:]:
        total = total + value.astype(F32)
    return total.astype(BF)


def gather_line(own):
    pieces = [own] + [None] * (NZ - 1)
    up = down = own
    for step in range(1, NZ // 2 + 1):
        up = expert_move(up, dz=-1)
        pieces[step] = up
        if step < NZ // 2:
            down = expert_move(down, dz=1)
            pieces[NZ - step] = down
    return pieces + [expert_move(piece, flip=True) for piece in pieces]


def scatter_line(own, other):
    arrived = expert_move(other, flip=True)

    def term(dz):
        return own[dz * 32 : dz * 32 + 32], arrived[dz * 32 : dz * 32 + 32]

    up = add(*term(NZ // 2))
    for dz in range(NZ // 2 - 1, 0, -1):
        up = add(expert_move(up, dz=1), *term(dz))
    down = add(*term(NZ // 2 + 1))
    for dz in range(NZ // 2 + 2, NZ):
        down = add(expert_move(down, dz=-1), *term(dz))
    return [expert_move(up, dz=1), expert_move(down, dz=-1), *term(0)]


def spread_dp(block):
    half = block.shape[0] // 2
    left = dp_move(block, 1)
    right = dp_move(block, -1)
    far_a = dp_move(left[:half], 1)
    far_b = dp_move(right[half:], -1)
    return [block, left, right, far_a, far_b]


def sum_dp(parts):
    own, left_a, left_b, right_a, right_b, far_a, far_b = parts
    from_a = dp_move(far_a, -1)
    from_b = dp_move(far_b, 1)
    got_left_b = dp_move(left_b, -1)
    got_right_a = dp_move(right_a, 1)
    got_left_a = dp_move(add(left_a, from_a), -1)
    got_right_b = dp_move(add(right_b, from_b), 1)
    half = own.shape[0] // 2
    result = []
    for j in range(NY):
        low = j * PIECE
        if low < half:
            terms = (got_left_a[low : low + PIECE], got_right_a[low : low + PIECE])
        else:
            at = low - half
            terms = (got_left_b[at : at + PIECE], got_right_b[at : at + PIECE])
        result.append(add(own[low : low + PIECE], *terms))
    return result


def per_device(
    tokens,
    routes,
    route_weight,
    gate_weight,
    up_weight,
    down_weight,
    gate_scale,
    up_scale,
    down_scale,
):
    rows, depth = tokens.shape
    top = routes.shape[1]
    experts = gate_weight.shape[0] * NY * NZ * NC
    all_rows = rows * NX * NY * NZ * NC
    place = lax.axis_index("expert")
    y, line = place // (NZ * NC), place % (NZ * NC)

    high = lax.reduce_precision(route_weight, 8, 7)
    low = lax.reduce_precision(route_weight - high, 8, 7)
    meta = jnp.concatenate(
        [routes.astype(BF), high.astype(BF), low.astype(BF), jnp.zeros((rows, META - 3 * top), BF)],
        axis=1,
    )
    pieces = gather_line(jnp.concatenate([tokens, meta], axis=1))

    lane = jnp.arange(META, dtype=jnp.int32)
    lane_expert = ((((y + lane % NY) % NY) * (NZ * NC) + line) * 2 + lane // NY).astype(F32)
    lanes = jnp.broadcast_to(jnp.where(lane < 8, lane_expert, -1.0)[None], (8, META))
    *blocks, counts = gather_rows(lanes, pieces, depth)

    weights = (
        gate_weight,
        up_weight,
        down_weight,
        jnp.repeat(gate_scale, BLOCK, axis=2),
        jnp.repeat(up_scale, BLOCK, axis=2),
        jnp.repeat(down_scale, BLOCK, axis=2),
    )
    half = NY * PIECE // 2
    parts = []
    for which in range(2):
        group = blocks[which * NY : (which + 1) * NY]
        group = [group[0]] + [expert_move(group[d], dy=d) for d in range(1, NY)]
        spread = spread_dp(jnp.concatenate(group, axis=0))
        parts.append(ffn(spread, [2 * half] + [half] * 6, which, weights))

    counts = counts + expert_move(counts, xor_y=1)
    counts = counts + expert_move(counts, xor_y=2)
    counts = counts + dp_move(counts, xor_x=1)
    counts = counts + dp_move(counts, xor_x=2)
    load_totals = counts[0, :experts]
    load_share = load_totals * (experts / (all_rows * top))
    label = jnp.arange(experts, dtype=jnp.int32)
    order = load_totals.astype(jnp.int32) * experts + (experts - 1 - label)
    first = experts - 1 - jnp.max(order) % experts
    second = experts - 1 - jnp.max(jnp.where(label == first, -1, order)) % experts
    hot = jnp.stack([first, second])

    named = routes[:, :, None] == hot[None, None, :]
    named_row = jnp.any(named, axis=1)
    before = jnp.arange(rows)[:, None] >= jnp.arange(rows)[None, :]
    upto = jnp.sum((before[:, :, None] & named_row[None, :, :]).astype(jnp.int32), axis=1)
    extra = named_row & (upto == CAP + 1)
    extra_weight = jnp.where(extra, jnp.sum(jnp.where(named, route_weight[:, :, None], 0.0), axis=1), 0.0)
    extra_rows = jnp.einsum(
        "tj,td->jd", extra.astype(BF), tokens, preferred_element_type=F32
    ).astype(BF)
    extra_rows = lax.all_gather(extra_rows, "dp", axis=0, tiled=True)
    extra_rows = lax.all_gather(extra_rows, "expert", axis=0, tiled=True)
    extra_parts = [
        ffn(
            [extra_rows],
            [extra_rows.shape[0]],
            which,
            weights,
            (hot == place * 2 + which).astype(jnp.int32),
        )[0]
        for which in range(2)
    ]
    extra_out = extra_parts[0] + extra_parts[1]
    extra_out = lax.psum_scatter(extra_out, "expert", scatter_dimension=0, tiled=True)
    extra_out = lax.psum_scatter(extra_out, "dp", scatter_dimension=0, tiled=True).astype(F32)

    returned = []
    for which in range(2):
        group = sum_dp(parts[which])
        returned += [group[0]] + [expert_move(group[d], dy=-d) for d in range(1, NY)]
    terms = scatter_line(*scatter_rows(lanes, pieces, returned, depth))
    total = terms[0].astype(F32)
    for term in terms[1:]:
        total = total + term.astype(F32)
    for j in range(2):
        total = total + extra_weight[:, j : j + 1] * extra_out[j : j + 1]
    return total.astype(BF), load_share


def solution(mesh):
    in_specs = (
        P(("dp", "expert"), None),
        P(("dp", "expert"), None),
        P(("dp", "expert"), None),
        P("expert", None, "dp"),
        P("expert", None, "dp"),
        P("expert", "dp", None),
        P("expert", None, "dp"),
        P("expert", None, "dp"),
        P("expert", "dp", None),
    )
    out_specs = (P(("dp", "expert"), None), P())
    return jax.shard_map(
        per_device, mesh=mesh, in_specs=in_specs, out_specs=out_specs, check_vma=False
    )
```

time: 662 us -> 528 us (0.80)
  blocking collectives: 170 us -> 37.9 us
  local copies, waits for them, and re-layouts: 114 us -> 19.8 us
  starting transfers between devices: 11.3 us -> 84.5 us
  Pallas kernels: 0 us -> 65.5 us
  matrix products: 34.6 us -> 0.14 us
  waiting for transfers between devices: 299 us -> 276 us
  other arithmetic: 6.17 us -> 15.8 us
    ppermute x0 -> x59, waiting for transfers between devices: none -> 170 us  [the longest x22 92.2 us: dp_move(): lax.ppermute(value, 'dp', [(x, (x + dx) % NX ^ xor_x) for x in range(NX)])]
    all_to_all x1 -> x0, blocking collectives: 91.7 us -> none  [send_out(): lax.all_to_all(buffer, 'expert', split_axis=0, concat_axis=2, tiled=True)]
    ppermute x0 -> x59, starting transfers between devices: none -> 84.4 us  [the longest x37 55.1 us: expert_move(): return lax.ppermute(value, 'expert', pairs)]
    all_to_all x1 -> x0, waiting for transfers between devices: 82.9 us -> none  [send_back(): lax.all_to_all(result, 'expert', split_axis=2, concat_axis=0, tiled=True)]
    all_gather x1, waiting for transfers between devices: 81.2 us -> 0.02 us  [per_device(): extra_rows = lax.all_gather(extra_rows, 'expert', axis=0, tiled=True)]
    psum x1 -> x0, blocking collectives: 78.5 us -> none  [per_device(): load_totals = lax.psum(jnp.sum(per_row, axis=0), ('dp', 'expert'))]
    pallas_call x0 -> x6, Pallas kernels: none -> 65.5 us  [the longest x4 52.5 us: ffn(): pl.pallas_call(functools.partial(ffn_kernel, in_rows, out_rows, steps, ma...]
    mul x6 -> x1, local copies, waits for them, and re-layouts: 47 us -> 0.01 us  [per_device(): total = total + extra_weight[:, j:j + 1] * extra_out[j:j + 1]]
  transfers between devices with their start and end apart: 3 -> 61, of which waited for: 3 -> 30; matrix products, arithmetic and copies ran while one was open for 8% -> 4% of each run, Pallas kernels for 0% -> 12%
where the time goes in v1:
time: 528 us; the launch traced here: 520 us
  waiting for transfers between devices  276 us (52%)
  starting transfers between devices  84.5 us (16%)
  Pallas kernels  65.5 us (12%)
  blocking collectives  37.9 us (7%)
  local copies, waits for them, and re-layouts  19.8 us (4%)
  between operations  19.8 us (4%)
  other arithmetic  15.8 us (3%)
    reduce_scatter x1, waiting for transfers between devices, per_device(): lax.psum_scatter(extra_out, 'expert', scatter_dimension=0, tiled=True)  107 us
    ppermute x22, waiting for transfers between devices, dp_move(): lax.ppermute(value, 'dp', [(x, (x + dx) % NX ^ xor_x) for x in range(NX)])  92.2 us
    ppermute x37, waiting for transfers between devices, expert_move(): return lax.ppermute(value, 'expert', pairs)  77.4 us
    ppermute x37, starting transfers between devices, expert_move(): return lax.ppermute(value, 'expert', pairs)  55.1 us
    pallas_call x4, Pallas kernels, ffn(): pl.pallas_call(functools.partial(ffn_kernel, in_rows, out_rows, steps, ma...  52.5 us
    ppermute x22, starting transfers between devices, dp_move(): lax.ppermute(value, 'dp', [(x, (x + dx) % NX ^ xor_x) for x in range(NX)])  29.4 us
    all_gather x1, blocking collectives, per_device(): extra_rows = lax.all_gather(extra_rows, 'dp', axis=0, tiled=True)  19.9 us
    unnamed x1, blocking collectives  18 us
  transfers between devices with their start and end apart: 61, of which 30 were waited for; matrix products, arithmetic and copies ran while one was open for 4% of the time, Pallas kernels for 12%

profile of v1, /device:TPU:8, one launch (start us, length us, event | category | flops | bytes accessed | tf_op | source)
XLA Modules:
  0.0 519.8 jit_solution(6080898006289535067)
XLA Ops:
  10.6 5.9 %collective-permute-start = (bf16[32,3712]{1,0:T(8,128)(2,1)S(1)}, bf16[32,3712]{1,0:T(8,128)(2,1)S(1)}, u32[]{:S(2)}, u32[]{:S(2)}) collective-permute-start(bf16[32,3712]{1,0:T(8,128)(2,1)S(1)} %concatenate.9.refs_0_), channel_id=1, source_target_pairs={{0,14},{1,15},{2,0},{3,1},{4,2},{5,3},{6,4},{7,5},{8,6},{9,7},{10,... | collective-permute-start | bytes 712712 | tf_op jit(solution)/shard_map/ppermute | solution.py:31
  16.5 5.0 collective-permute-done.refs_1_
  46.1 4.4 gather_rows.1
  59.9 7.8 %collective-permute-done.15 = bf16[48,3584]{1,0:T(8,128)(2,1)S(1)} collective-permute-done((bf16[48,3584]{1,0:T(8,128)(2,1)S(1)}, bf16[48,3584]{1,0:T(8,128)(2,1)S(1)}, u32[]{:S(2)}, u32[]{:S(2)}) %collective-permute-start.15) | collective-permute-done | bytes 344096 | tf_op jit(solution)/shard_map/ppermute | solution.py:31
  67.8 4.5 collective-permute-done.17
  80.3 4.8 collective-permute-done.33
  89.1 17.6 %collective-permute-done.18.refs_1_ = bf16[192,3584]{1,0:T(8,128)(2,1)S(1)} collective-permute-done((bf16[192,3584]{1,0:T(8,128)(2,1)S(1)}, bf16[192,3584]{1,0:T(8,128)(2,1)S(1)}, u32[]{:S(2)}, u32[]{:S(2)}) %collective-permute-start.18) | collective-permute-done | bytes 1376288 | tf_op jit(solution)/shard_map/ppermute | solution.py:35
  120.8 26.7 %collective-permute-done.57 = f32[8,128]{1,0:T(8,128)S(1)} collective-permute-done((f32[8,128]{1,0:T(8,128)S(1)}, f32[8,128]{1,0:T(8,128)S(1)}, u32[]{:S(2)}, u32[]{:S(2)}) %collective-permute-start.57) | collective-permute-done | bytes 4128 | tf_op jit(solution)/shard_map/ppermute | solution.py:35
  165.1 14.3 %ffn.4 = (bf16[192,3584]{1,0:T(8,128)(2,1)}, bf16[96,3584]{1,0:T(8,128)(2,1)S(1)}, bf16[96,3584]{1,0:T(8,128)(2,1)S(1)}, bf16[96,3584]{1,0:T(8,128)(2,1)S(1)}, b...) custom-call(bf16[192,3584]{1,0:T(8,128)(2,1)} %copy-done.34, ...), custom_call_target="tpu_custom_call" | custom-call | flops 4227858432 | bytes 16515072 | tf_op jit(solution)/shard_map/ffn/pallas_call | solution.py:232
  184.1 19.9 %all-gather = bf16[4,2,3584]{2,1,0:T(2,128)(2,1)S(1)} all-gather(bf16[1,2,3584]{2,1,0:T(2,128)(2,1)S(1)} %fusion), channel_id=1, replica_groups=mesh['dp'=4,'expert'=64] {'dp'}, dimensions={0}, use_global_device_ids=true | all-gather | bytes 71680 | tf_op jit(solution)/shard_map/all_gather | solution.py:385
  208.1 14.3 %ffn.5 = (bf16[192,3584]{1,0:T(8,128)(2,1)}, bf16[96,3584]{1,0:T(8,128)(2,1)S(1)}, bf16[96,3584]{1,0:T(8,128)(2,1)S(1)}, bf16[96,3584]{1,0:T(8,128)(2,1)S(1)}, b...) custom-call(bf16[192,3584]{1,0:T(8,128)(2,1)} %constant_dynamic-update-slice_fusion.4.refs_0_, ...), custom_call_target="tpu_custom_call" | custom-call | flops 4227858432 | bytes 16515072 | tf_op jit(solution)/shard_map/ffn/pallas_call | solution.py:232
  226.9 11.2 %collective-permute-done.22 = bf16[96,3584]{1,0:T(8,128)(2,1)S(1)} collective-permute-done((bf16[96,3584]{1,0:T(8,128)(2,1)}, bf16[96,3584]{1,0:T(8,128)(2,1)S(1)}, u32[]{:S(2)}, u32[]{:S(2)}) %collective-permute-start.22) | collective-permute-done | bytes 688160 | tf_op jit(solution)/shard_map/ppermute | solution.py:35
  240.7 24.1 %collective-permute-done.38 = bf16[96,3584]{1,0:T(8,128)(2,1)S(1)} collective-permute-done((bf16[96,3584]{1,0:T(8,128)(2,1)S(1)}, bf16[96,3584]{1,0:T(8,128)(2,1)S(1)}, u32[]{:S(2)}, u32[]{:S(2)}) %collective-permute-start.38) | collective-permute-done | bytes 688160 | tf_op jit(solution)/shard_map/ppermute | solution.py:35
  270.3 10.4 %collective-permute-done.23 = bf16[96,3584]{1,0:T(8,128)(2,1)S(1)} collective-permute-done((bf16[96,3584]{1,0:T(8,128)(2,1)S(1)}, bf16[96,3584]{1,0:T(8,128)(2,1)S(1)}, u32[]{:S(2)}, u32[]{:S(2)}) %collective-permute-start.23) | collective-permute-done | bytes 688160 | tf_op jit(solution)/shard_map/ppermute | solution.py:35
  284.3 4.6 collective-permute-start.29
  299.1 5.3 %collective-permute-done.29.refs_18_ = bf16[48,3584]{1,0:T(8,128)(2,1)S(1)} collective-permute-done((bf16[48,3584]{1,0:T(8,128)(2,1)S(1)}, bf16[48,3584]{1,0:T(8,128)(2,1)S(1)}, u32[]{:S(2)}, u32[]{:S(2)}) %collective-permute-start.29) | collective-permute-done | bytes 344096 | tf_op jit(solution)/shard_map/ppermute | solution.py:31
  306.8 5.0 collective-permute-done.45.refs_22_
  314.8 8.6 %scatter_rows.1 = (bf16[256,3584]{1,0:T(8,128)(2,1)}, bf16[256,3584]{1,0:T(8,128)(2,1)}) custom-call(f32[8,128]{1,0:T(8,128)S(1)} %broadcast_in_dim.48.lanes_ref, bf16[32,3712]{1,0:T(8,128)(2,1)S(1)} %concatenate.9.refs_0_, bf16[32,3712]{1,0:T(8,128)(2,1)S(1)} %collective-permute-done.refs_1_, bf16[32,3712]{1,0:T(8,128)(2,1)S(1)} %copy-done.10, ...), custom_call_target="tpu_custom_call" | custom-call | flops 2818572288 | bytes 10485760 | tf_op jit(solution)/shard_map/scatter_rows/pallas_call | solution.py:142
  323.4 11.9 %ffn.6 = bf16[512,3584]{1,0:T(8,128)(2,1)S(1)} custom-call(s32[2]{0:T(128)S(1)} %compare_convert_fusion.1.refs_0_, bf16[512,3584]{1,0:T(8,128)(2,1)} %all-gather.3.cloned.1.call-done.refs_1_, bf16[2,3584,256]{2,1,0:T(8,128)(2,1)} %refs_2_.3, bf16[2,3584,256]{2,1,0:T(8,128)(2,1)} %refs_3_.3, bf16[2,256,3584]{2,1,0:T(8,128)(2,1)} %refs_4_.3, ...), custom_call_target="tpu_custom_call" | custom-call | flops 2818572288 | bytes 12845056 | tf_op jit(solution)/shard_map/ffn/pallas_call | solution.py:232
  335.3 11.9 %ffn.7 = bf16[512,3584]{1,0:T(8,128)(2,1)S(1)} custom-call(s32[2]{0:T(128)S(1)} %get-tuple-element.54.refs_0_, bf16[512,3584]{1,0:T(8,128)(2,1)} %all-gather.3.cloned.1.call-done.refs_1_, bf16[2,3584,256]{2,1,0:T(8,128)(2,1)} %refs_2_.3, bf16[2,3584,256]{2,1,0:T(8,128)(2,1)} %refs_3_.3, bf16[2,256,3584]{2,1,0:T(8,128)(2,1)} %refs_4_.3, ...), custom_call_target="tpu_custom_call" | custom-call | flops 2818572288 | bytes 12845056 | tf_op jit(solution)/shard_map/ffn/pallas_call | solution.py:232
  353.9 8.6 %collective-permute-done.48 = bf16[32,3584]{1,0:T(8,128)(2,1)S(1)} collective-permute-done((bf16[32,3584]{1,0:T(8,128)(2,1)S(1)}, bf16[32,3584]{1,0:T(8,128)(2,1)S(1)}, u32[]{:S(2)}, u32[]{:S(2)}) %collective-permute-start.48) | collective-permute-done | bytes 229408 | tf_op jit(solution)/shard_map/ppermute | solution.py:31
  367.2 5.3 %collective-permute-done.49 = bf16[32,3584]{1,0:T(8,128)(2,1)S(1)} collective-permute-done((bf16[32,3584]{1,0:T(8,128)(2,1)S(1)}, bf16[32,3584]{1,0:T(8,128)(2,1)S(1)}, u32[]{:S(2)}, u32[]{:S(2)}) %collective-permute-start.49) | collective-permute-done | bytes 229408 | tf_op jit(solution)/shard_map/ppermute | solution.py:31
  385.8 106.7 %reduce-scatter.2.cloned.1.call-done = bf16[8,3584]{1,0:T(8,128)(2,1)} async-done(((bf16[512,3584]{1,0:T(8,128)(2,1)}), bf16[8,3584]{1,0:T(8,128)(2,1)}) %reduce-scatter.2.cloned.1.call-update) | async-done | bytes 57360 | tf_op jit(solution)/shard_map/reduce_scatter | solution.py:398
  492.5 18.0 %all-reduce = bf16[8,3584]{1,0:T(8,128)(2,1)S(1)} all-reduce(bf16[8,3584]{1,0:T(8,128)(2,1)} %reduce-scatter.2.cloned.1.call-done), channel_id=3, replica_groups=mesh['dp'=4,'expert'=64] {'dp'}, use_global_device_ids=true, to_apply=%region_6.7.clone | all-reduce | flops 28672 | bytes 114688
  (266 shorter events, 143.2 us)
Async XLA Ops:
  7.2 316.2 %all-gather.3.cloned.1.call-start = ((), (), s32[]{:S(2)}) async-start(), calls=%async_computation.1 | async-start | bytes 3727360 | tf_op jit(solution)/shard_map/all_gather | solution.py:386
  72.3 34.4 %collective-permute-start.18 = (bf16[192,3584]{1,0:T(8,128)(2,1)S(1)}, bf16[192,3584]{1,0:T(8,128)(2,1)S(1)}, u32[]{:S(2)}, u32[]{:S(2)}) collective-permute-start(bf16[192,3584]{1,0:T(8,128)(2,1)S(1)} %constant_dynamic-update-slice_fusion.refs_0_), channel_id=1, source_target_pairs={{0,64},{64,128},{128,192},{192,0},{1,65},{65,129},{129,193},{193,1... | collective-permute-start | bytes 4128776 | tf_op jit(solution)/shard_map/ppermute | solution.py:35
  73.8 34.1 %collective-permute-start.19 = (bf16[192,3584]{1,0:T(8,128)(2,1)S(1)}, bf16[192,3584]{1,0:T(8,128)(2,1)S(1)}, u32[]{:S(2)}, u32[]{:S(2)}) collective-permute-start(bf16[192,3584]{1,0:T(8,128)(2,1)S(1)} %constant_dynamic-update-slice_fusion.refs_0_), channel_id=1, source_target_pairs={{0,192},{64,0},{128,64},{192,128},{1,193},{65,1},{129,65},{193,129... | collective-permute-start | bytes 4128776 | tf_op jit(solution)/shard_map/ppermute | solution.py:35
  85.8 72.0 %collective-permute-start.34 = (bf16[192,3584]{1,0:T(8,128)(2,1)}, bf16[192,3584]{1,0:T(8,128)(2,1)S(1)}, u32[]{:S(2)}, u32[]{:S(2)}) collective-permute-start(bf16[192,3584]{1,0:T(8,128)(2,1)} %constant_dynamic-update-slice_fusion.4.refs_0_), channel_id=1, source_target_pairs={{0,64},{64,128},{128,192},{192,0},{1,65},{65,129},{129,193},{193,1... | collective-permute-start | bytes 4128776 | tf_op jit(solution)/shard_map/ppermute | solution.py:35
  87.3 72.7 %collective-permute-start.35 = (bf16[192,3584]{1,0:T(8,128)(2,1)}, bf16[192,3584]{1,0:T(8,128)(2,1)}, u32[]{:S(2)}, u32[]{:S(2)}) collective-permute-start(bf16[192,3584]{1,0:T(8,128)(2,1)} %constant_dynamic-update-slice_fusion.4.refs_0_), channel_id=1, source_target_pairs={{0,192},{64,0},{128,64},{192,128},{1,193},{65,1},{129,65},{193,129... | collective-permute-start | bytes 4128776 | tf_op jit(solution)/shard_map/ppermute | solution.py:35
  107.6 57.5 %collective-permute-start.20 = (bf16[96,3584]{1,0:T(8,128)(2,1)}, bf16[96,3584]{1,0:T(8,128)(2,1)S(1)}, u32[]{:S(2)}, u32[]{:S(2)}) collective-permute-start(bf16[96,3584]{1,0:T(8,128)(2,1)} %slice.196), channel_id=1, source_target_pairs={{0,64},{64,128},{128,192},{192,0},{1,65},{65,129},{129,193},{193,1... | collective-permute-start | bytes 2064392 | tf_op jit(solution)/shard_map/ppermute | solution.py:35
  108.9 56.2 %collective-permute-start.21 = (bf16[96,3584]{1,0:T(8,128)(2,1)}, bf16[96,3584]{1,0:T(8,128)(2,1)S(1)}, u32[]{:S(2)}, u32[]{:S(2)}) collective-permute-start(bf16[96,3584]{1,0:T(8,128)(2,1)} %slice.197), channel_id=1, source_target_pairs={{0,192},{64,0},{128,64},{192,128},{1,193},{65,1},{129,65},{193,129... | collective-permute-start | bytes 2064392 | tf_op jit(solution)/shard_map/ppermute | solution.py:35
  120.8 26.7 %collective-permute-start.57 = (f32[8,128]{1,0:T(8,128)S(1)}, f32[8,128]{1,0:T(8,128)S(1)}, u32[]{:S(2)}, u32[]{:S(2)}) collective-permute-start(f32[8,128]{1,0:T(8,128)S(1)} %add.241), channel_id=1, source_target_pairs={{0,64},{64,0},{128,192},{192,128},{1,65},{65,1},{129,193},{193,129... | collective-permute-start | bytes 12296 | tf_op jit(solution)/shard_map/ppermute | solution.py:35
  159.9 46.9 %collective-permute-start.36 = (bf16[96,3584]{1,0:T(8,128)(2,1)}, bf16[96,3584]{1,0:T(8,128)(2,1)S(1)}, u32[]{:S(2)}, u32[]{:S(2)}) collective-permute-start(bf16[96,3584]{1,0:T(8,128)(2,1)} %slice.206), channel_id=1, source_target_pairs={{0,64},{64,128},{128,192},{192,0},{1,65},{65,129},{129,193},{193,1... | collective-permute-start | bytes 2064392 | tf_op jit(solution)/shard_map/ppermute | solution.py:35
  162.1 46.0 %collective-permute-start.37 = (bf16[96,3584]{1,0:T(8,128)(2,1)}, bf16[96,3584]{1,0:T(8,128)(2,1)S(1)}, u32[]{:S(2)}, u32[]{:S(2)}) collective-permute-start(bf16[96,3584]{1,0:T(8,128)(2,1)} %slice.207), channel_id=1, source_target_pairs={{0,192},{64,0},{128,64},{192,128},{1,193},{65,1},{129,65},{193,129... | collective-permute-start | bytes 2064392 | tf_op jit(solution)/shard_map/ppermute | solution.py:35
  183.7 39.4 %collective-permute-start.27 = (bf16[96,3584]{1,0:T(8,128)(2,1)}, bf16[96,3584]{1,0:T(8,128)(2,1)}, u32[]{:S(2)}, u32[]{:S(2)}) collective-permute-start(bf16[96,3584]{1,0:T(8,128)(2,1)} %get-tuple-element.37), channel_id=1, source_target_pairs={{0,64},{64,128},{128,192},{192,0},{1,65},{65,129},{129,193},{193,1... | collective-permute-start | bytes 2064392 | tf_op jit(solution)/shard_map/ppermute | solution.py:35
  204.6 287.9 %reduce-scatter.2.cloned.1.call-start = ((), (), s32[]{:S(2)}) async-start(), calls=%async_computation.2 | async-start | bytes 3727360 | tf_op jit(solution)/shard_map/reduce_scatter | solution.py:398
  204.7 60.3 %collective-permute-start.26 = (bf16[96,3584]{1,0:T(8,128)(2,1)}, bf16[96,3584]{1,0:T(8,128)(2,1)S(1)}, u32[]{:S(2)}, u32[]{:S(2)}) collective-permute-start(bf16[96,3584]{1,0:T(8,128)(2,1)} %copy-done.5), channel_id=1, source_target_pairs={{0,192},{64,0},{128,64},{192,128},{1,193},{65,1},{129,65},{193,129... | collective-permute-start | bytes 2064392 | tf_op jit(solution)/shard_map/ppermute | solution.py:35
  204.8 62.3 %collective-permute-start.24 = (bf16[96,3584]{1,0:T(8,128)(2,1)}, bf16[96,3584]{1,0:T(8,128)(2,1)S(1)}, u32[]{:S(2)}, u32[]{:S(2)}) collective-permute-start(bf16[96,3584]{1,0:T(8,128)(2,1)} %copy-done.4), channel_id=1, source_target_pairs={{0,64},{64,128},{128,192},{192,0},{1,65},{65,129},{129,193},{193,1... | collective-permute-start | bytes 2064392 | tf_op jit(solution)/shard_map/ppermute | solution.py:35
  206.8 31.3 %collective-permute-start.22 = (bf16[96,3584]{1,0:T(8,128)(2,1)}, bf16[96,3584]{1,0:T(8,128)(2,1)S(1)}, u32[]{:S(2)}, u32[]{:S(2)}) collective-permute-start(bf16[96,3584]{1,0:T(8,128)(2,1)} %copy-done.6), channel_id=1, source_target_pairs={{0,192},{64,0},{128,64},{192,128},{1,193},{65,1},{129,65},{193,129... | collective-permute-start | bytes 2064392 | tf_op jit(solution)/shard_map/ppermute | solution.py:35
  223.1 61.2 %collective-permute-start.42 = (bf16[96,3584]{1,0:T(8,128)(2,1)S(1)}, bf16[96,3584]{1,0:T(8,128)(2,1)S(1)}, u32[]{:S(2)}, u32[]{:S(2)}) collective-permute-start(bf16[96,3584]{1,0:T(8,128)(2,1)S(1)} %get-tuple-element.46), channel_id=1, source_target_pairs={{0,192},{64,0},{128,64},{192,128},{1,193},{65,1},{129,65},{193,129... | collective-permute-start | bytes 2064392 | tf_op jit(solution)/shard_map/ppermute | solution.py:35
  238.1 26.7 %collective-permute-start.38 = (bf16[96,3584]{1,0:T(8,128)(2,1)S(1)}, bf16[96,3584]{1,0:T(8,128)(2,1)S(1)}, u32[]{:S(2)}, u32[]{:S(2)}) collective-permute-start(bf16[96,3584]{1,0:T(8,128)(2,1)S(1)} %get-tuple-element.44), channel_id=1, source_target_pairs={{0,192},{64,0},{128,64},{192,128},{1,193},{65,1},{129,65},{193,129... | collective-permute-start | bytes 2064392 | tf_op jit(solution)/shard_map/ppermute | solution.py:35
  240.3 26.9 %collective-permute-start.28 = (bf16[96,3584]{1,0:T(8,128)(2,1)S(1)}, bf16[96,3584]{1,0:T(8,128)(2,1)S(1)}, u32[]{:S(2)}, u32[]{:S(2)}) collective-permute-start(bf16[96,3584]{1,0:T(8,128)(2,1)S(1)} %add_convert_fusion.2), channel_id=1, source_target_pairs={{0,64},{64,128},{128,192},{192,0},{1,65},{65,129},{129,193},{193,1... | collective-permute-start | bytes 2064392 | tf_op jit(solution)/shard_map/ppermute | solution.py:35
  265.0 23.9 %collective-permute-start.40 = (bf16[96,3584]{1,0:T(8,128)(2,1)S(1)}, bf16[96,3584]{1,0:T(8,128)(2,1)S(1)}, u32[]{:S(2)}, u32[]{:S(2)}) collective-permute-start(bf16[96,3584]{1,0:T(8,128)(2,1)S(1)} %get-tuple-element.45), channel_id=1, source_target_pairs={{0,64},{64,128},{128,192},{192,0},{1,65},{65,129},{129,193},{193,1... | collective-permute-start | bytes 2064392 | tf_op jit(solution)/shard_map/ppermute | solution.py:35
  267.1 24.3 %collective-permute-start.44 = (bf16[96,3584]{1,0:T(8,128)(2,1)S(1)}, bf16[96,3584]{1,0:T(8,128)(2,1)S(1)}, u32[]{:S(2)}, u32[]{:S(2)}) collective-permute-start(bf16[96,3584]{1,0:T(8,128)(2,1)S(1)} %add_convert_fusion), channel_id=1, source_target_pairs={{0,64},{64,128},{128,192},{192,0},{1,65},{65,129},{129,193},{193,1... | collective-permute-start | bytes 2064392 | tf_op jit(solution)/shard_map/ppermute | solution.py:35
  267.2 24.2 %collective-permute-start.39 = (bf16[96,3584]{1,0:T(8,128)(2,1)S(1)}, bf16[96,3584]{1,0:T(8,128)(2,1)S(1)}, u32[]{:S(2)}, u32[]{:S(2)}) collective-permute-start(bf16[96,3584]{1,0:T(8,128)(2,1)S(1)} %add_convert_fusion.1), channel_id=1, source_target_pairs={{0,192},{64,0},{128,64},{192,128},{1,193},{65,1},{129,65},{193,129... | collective-permute-start | bytes 2064392 | tf_op jit(solution)/shard_map/ppermute | solution.py:35
  323.3 26.8 %collective-permute-start.47 = (bf16[256,3584]{1,0:T(8,128)(2,1)}, bf16[256,3584]{1,0:T(8,128)(2,1)}, u32[]{:S(2)}, u32[]{:S(2)}) collective-permute-start(bf16[256,3584]{1,0:T(8,128)(2,1)} %get-tuple-element.50), channel_id=1, source_target_pairs={{0,1},{1,0},{2,3},{3,2},{4,5},{5,4},{6,7},{7,6},{8,9},{9,8},{10,11... | collective-permute-start | bytes 5505032 | tf_op jit(solution)/shard_map/ppermute | solution.py:31
  382.8 127.9 %collective-permute-start.54 = (bf16[32,3584]{1,0:T(8,128)(2,1)S(1)}, bf16[32,3584]{1,0:T(8,128)(2,1)S(1)}, u32[]{:S(2)}, u32[]{:S(2)}) collective-permute-start(bf16[32,3584]{1,0:T(8,128)(2,1)S(1)} %get-tuple-element.57), channel_id=1, source_target_pairs={{0,14},{1,15},{2,0},{3,1},{4,2},{5,3},{6,4},{7,5},{8,6},{9,7},{10,... | collective-permute-start | bytes 688136 | tf_op jit(solution)/shard_map/ppermute | solution.py:31
  385.8 124.9 %collective-permute-start.51 = (bf16[32,3584]{1,0:T(8,128)(2,1)S(1)}, bf16[32,3584]{1,0:T(8,128)(2,1)S(1)}, u32[]{:S(2)}, u32[]{:S(2)}) collective-permute-start(bf16[32,3584]{1,0:T(8,128)(2,1)S(1)} %get-tuple-element.56), channel_id=1, source_target_pairs={{0,2},{1,3},{2,4},{3,5},{4,6},{5,7},{6,8},{7,9},{8,10},{9,11},{10,... | collective-permute-start | bytes 688136 | tf_op jit(solution)/shard_map/ppermute | solution.py:31
  (84 other events, 1214.6 us)
Sparse Core Ops, SparseCore 0:
  204.8 78.2 all-gather.2
  350.2 142.3 reduce-scatter.1
